TPU v7x, 32 devices: a whole 2x2x4 slice. The times are simulated.
32 devices in a mesh: seq: 4 (over y, x), exp: 8 (over z, core).
Axes of the slice: x: 2, y: 2, z: 4, core: 2. Of those that a mesh axis runs over, the one named last changes fastest.
Arguments:
- resid: bfloat16 [8, 384, 2048], P('exp', 'seq'), may hold values from -6 to 6
- qkv: bfloat16 [8, 384, 6144], P('exp', 'seq'), may hold values from -8 to 8
- w_out: bfloat16 [2048, 2048], P('seq'), may hold values from -0.125 to 0.125
- norm_gain: float32 [2048], replicated, may hold values from 0.1 to 1.9
- router_w: bfloat16 [2048, 64], replicated, may hold values from -0.125 to 0.125
- expert_ids: int32 [8, 384, 6], P('exp'), may hold values from 0 to 63, all different within a row; in each aligned block of 96 rows (0 to 95, 96 to 191, ..., all dimensions but the last counted through in order) at most 12 rows name the same one
- w_gate_up: bfloat16 [64, 2048, 2, 1408], P('exp', None, None, 'seq'), may hold values from -0.125 to 0.125
- w_down: bfloat16 [64, 1408, 2048], P('exp', 'seq'), may hold values from -0.15625 to 0.15625
Outputs:
- layer_out: bfloat16 [8, 384, 2048], P('exp', 'seq')
Inputs may be any that keep to these rules, and one draw needn't show every extreme that they name: `expert_ids`: each point names 6 different experts. In each aligned block of 96 points (the points of one device, in the order of sets and then points), no expert is named by more than 12 points, and in every draw some expert is named by exactly 12 points of some block.
All inputs are finite; a program needn't handle non-finite values.
Results may differ from a plain program's by a relative error of at most 0.0065.
Values may be sent and summed in bfloat16 or wider, within the bound.
A program may use at most 128 MiB of HBM per device.

v0:
```python
import math

import jax
import jax.numpy as jnp
from jax import lax
from jax.sharding import PartitionSpec as P

H = 16
HD = 128
EXPERTS = 64


epsilon = 1e-05


def gate_weights(normed_rows, router_w, chosen):
    logits = jnp.dot(normed_rows, router_w, preferred_element_type=jnp.float32)
    match = chosen[:, :, None] == jnp.arange(logits.shape[1], dtype=jnp.int32)[None, None, :]
    picked = jnp.sum(jnp.where(match, logits[:, None, :], jnp.zeros((), logits.dtype)), axis=-1)
    squashed = jax.nn.sigmoid(picked)
    return squashed / jnp.sum(squashed, axis=-1, keepdims=True)


def slot_ranks(chosen, block_rows, experts):
    blocks = chosen.shape[0] // block_rows
    grouped = chosen.reshape(blocks, block_rows * chosen.shape[1])
    hits = (grouped[:, :, None] == jnp.arange(experts, dtype=jnp.int32)[None, None, :]).astype(
        jnp.int32
    )
    ranks = jnp.sum(jnp.cumsum(hits, axis=1) * hits, axis=-1) - 1
    return ranks.reshape(chosen.shape)


def expert_part(received, w_gate_up, w_down):
    both = jnp.einsum("aend,edgf->aengf", received, w_gate_up, preferred_element_type=jnp.float32)
    hidden = (jax.nn.silu(both[:, :, :, 0]) * both[:, :, :, 1]).astype(jnp.bfloat16)
    return jnp.einsum("aenf,efd->aend", hidden, w_down, preferred_element_type=jnp.float32)


def scatter_rows(normed_rows, slot_index, buffer_rows):
    feature_width = normed_rows.shape[1]
    spread = jnp.broadcast_to(
        normed_rows[:, None, :], (slot_index.shape[0], slot_index.shape[1], feature_width)
    )
    empty = jnp.zeros((buffer_rows, feature_width), jnp.bfloat16)
    return empty.at[slot_index.reshape(-1)].set(spread.reshape(-1, feature_width))


def combine_rows(out_table, slot_index, gate_vals):
    picked = out_table[slot_index].astype(jnp.float32)
    return jnp.sum(gate_vals[:, :, None] * picked, axis=1)


def on_device(resid, qkv, w_out, norm_gain, router_w, expert_ids, w_gate_up, w_down):
    row_count = resid.shape[1]
    model_width = resid.shape[2]
    seq_size = lax.axis_size("seq")
    exp_size = lax.axis_size("exp")
    seq_length = row_count * seq_size
    head_local = H // seq_size
    local_width = head_local * HD
    packed = qkv.reshape(row_count, 3, seq_size, local_width)
    regrouped = lax.all_to_all(packed, "seq", split_axis=2, concat_axis=0, tiled=True)
    queries = regrouped[:, 0, 0].reshape(seq_length, head_local, HD)
    keys_all = regrouped[:, 1, 0].reshape(seq_length, head_local, HD)
    values_all = regrouped[:, 2, 0].reshape(seq_length, head_local, HD)
    query_block = min(seq_length, 512)

    def attend_block(query_rows):
        scores = jnp.einsum(
            "qhd,khd->hqk", query_rows, keys_all, preferred_element_type=jnp.float32
        ) / math.sqrt(HD)
        weights = jax.nn.softmax(scores, axis=-1).astype(jnp.bfloat16)
        mixed_heads = jnp.einsum(
            "hqk,khd->qhd", weights, values_all, preferred_element_type=jnp.float32
        )
        return mixed_heads.reshape(query_rows.shape[0], local_width).astype(jnp.bfloat16)

    attended = lax.map(
        attend_block, queries.reshape(seq_length // query_block, query_block, head_local, HD)
    )
    attended = attended.reshape(seq_length, local_width)
    back = lax.all_to_all(
        attended.reshape(seq_length, 1, local_width), "seq", split_axis=0, concat_axis=1, tiled=True
    )
    point_rows = back.reshape(row_count, model_width)
    projected = jnp.dot(
        point_rows,
        lax.all_gather(w_out, "seq", axis=0, tiled=True),
        preferred_element_type=jnp.float32,
    )
    mixed = resid[0].astype(jnp.float32) + projected
    meansq = jnp.mean(mixed * mixed, axis=-1, keepdims=True)
    normed = (mixed * lax.rsqrt(meansq + epsilon) * norm_gain).astype(jnp.bfloat16)
    exp_local = w_gate_up.shape[0]
    slot_cap = row_count // 8
    gathered = lax.all_gather(normed, "seq", axis=0, tiled=True)
    chosen = expert_ids[0]
    gate_vals = gate_weights(gathered, router_w, chosen)
    ranks = slot_ranks(chosen, row_count, EXPERTS)
    owner_rows = seq_size * slot_cap
    source_block = (jnp.arange(seq_length, dtype=jnp.int32) // row_count)[:, None]
    slot_index = chosen * owner_rows + source_block * slot_cap + ranks
    outgoing = scatter_rows(gathered, slot_index, EXPERTS * owner_rows)
    outgoing = outgoing.reshape(exp_size, exp_local, owner_rows, model_width)
    partial_out = expert_part(
        lax.all_to_all(outgoing, "exp", split_axis=0, concat_axis=0, tiled=True), w_gate_up, w_down
    ).astype(jnp.bfloat16)
    returned = lax.all_to_all(partial_out, "exp", split_axis=0, concat_axis=0, tiled=True)
    out_table = returned.reshape(-1, model_width)
    expert_sum = lax.psum_scatter(
        combine_rows(out_table, slot_index, gate_vals).astype(jnp.bfloat16),
        "seq",
        scatter_dimension=0,
        tiled=True,
    ).astype(jnp.float32)
    return (mixed + expert_sum).astype(jnp.bfloat16).reshape(1, row_count, model_width)


def solution(mesh):
    in_specs = (
        P("exp", "seq", None),
        P("exp", "seq", None),
        P("seq", None),
        P(),
        P(),
        P("exp", None, None),
        P("exp", None, None, "seq"),
        P("exp", "seq", None),
    )
    out_specs = P("exp", "seq", None)
    return jax.shard_map(
        on_device, mesh=mesh, in_specs=in_specs, out_specs=out_specs, check_vma=False
    )
```

profile of v0, /device:TPU:0, one launch (start us, length us, event | category | flops | bytes accessed | tf_op | source)
XLA Modules:
  0.0 894.7 jit_solution(14497134732744187044)
XLA Ops:
  6.5 0.7 all-gather.3.cloned.1.call-update
  7.3 2.0 reshape.211
  9.3 0.2 copy.95
  9.5 27.1 %all_to_all.43 = bf16[96,3,4,512]{3,0,1,2:T(8,128)(2,1)S(1)} all-to-all(bf16[96,3,4,512]{3,0,1,2:T(8,128)(2,1)S(1)} %copy.95), channel_id=1, replica_groups=mesh['seq'=4,'exp'=8] {'seq'}, dimensions={2} | all-to-all | bytes 2359296 | tf_op jit(solution)/shard_map/all_to_all | solution.py:63
  36.8 0.2 copy.98
  37.0 0.2 copy.101
  37.3 0.2 copy.97
  37.5 2.3 fusion.38
  39.8 2.1 convolution_convert_fusion
  41.9 0.5 broadcast.205
  42.4 0.9 reduce.2
  43.3 0.2 copy.137
  43.5 0.3 reshape.245
  43.8 12.8 %all_to_all.44 = bf16[4,2,24576]{2,1,0:T(2,128)(2,1)S(1)} all-to-all(bf16[4,2,24576]{2,1,0:T(2,128)(2,1)S(1)} %reshape.245), channel_id=1, replica_groups=mesh['seq'=4,'exp'=8] {'seq'}, dimensions={0} | all-to-all | bytes 786432 | tf_op jit(solution)/shard_map/all_to_all | solution.py:83
  56.6 0.4 reshape.246
  57.0 0.3 copy.104
  57.5 51.9 %all-gather.3.cloned.1.call-done = bf16[2048,2048]{1,0:T(8,128)(2,1)} async-done(((bf16[512,2048]{1,0:T(8,128)(2,1)}), bf16[2048,2048]{1,0:T(8,128)(2,1)}) %all-gather.3.cloned.1.call-update) | async-done | bytes 8388624 | tf_op jit(solution)/shard_map/all_gather | solution.py:89
  109.4 5.0 multiply_reduce_fusion.2
  114.4 0.9 multiply_convert_fusion
  115.3 0.1 copy.106
  115.4 0.2 eq.41
  115.6 0.2 mul.85
  115.9 0.2 add.136
  116.2 6.0 reduce-window.6
  122.2 0.2 slice.37
  122.4 0.2 copy.109
  122.7 0.2 bitcast_bitcast_fusion
  123.2 23.2 %all-gather.5.cloned.1.call-done = bf16[384,2048]{1,0:T(8,128)(2,1)} async-done(((bf16[96,2048]{1,0:T(8,128)(2,1)}), bf16[384,2048]{1,0:T(8,128)(2,1)}) %all-gather.5.cloned.1.call-update) | async-done | bytes 1572880 | tf_op jit(solution)/shard_map/all_gather | solution.py:97
  146.4 7.0 broadcast_in_dim.26
  153.4 15.8 %reshape.233 = bf16[2304,2048]{1,0:T(8,128)(2,1)} reshape(bf16[384,6,2048]{2,1,0:T(8,128)(2,1)} %broadcast_in_dim.26) | data formatting | bytes 18874368 | tf_op jit(solution)/shard_map/reshape | solution.py:46
  169.2 23.8 %scatter_custom_fusion = bf16[3072,2048]{1,0:T(8,128)(2,1)} fusion(s32[2304]{0:T(1024)S(1)} %fusion.30, bf16[2304,2048]{1,0:T(8,128)(2,1)} %reshape.233, bf16[]{:T(256)} %constant.34.clone.1), kind=kCustom, calls=%fused_computation.10 | custom fusion | bytes 12583424 | tf_op jit(solution)/shard_map/scatter | solution.py:46
  193.1 281.0 %all_to_all.45 = bf16[8,8,48,2048]{3,2,1,0:T(8,128)(2,1)} all-to-all(bf16[8,8,48,2048]{3,2,1,0:T(8,128)(2,1)} %bitcast.97), channel_id=1, replica_groups=mesh['seq'=4,'exp'=8] {'exp'}, dimensions={0} | all-to-all | bytes 25165824 | tf_op jit(solution)/shard_map/all_to_all | solution.py:107
  474.1 22.3 %fusion.12 = f32[8,8,48,2,352]{4,2,3,0,1:T(8,128)} fusion(bf16[8,2048,2,352]{1,3,2,0:T(8,128)(2,1)} %param.14, bf16[8,8,48,2048]{3,2,1,0:T(8,128)(2,1)} %all_to_all.45), kind=kOutput, calls=%fused_computation.16 | convolution fusion | flops 8858370048 | bytes 44302336 | tf_op jit(solution)/shard_map/aend,edgf->aengf/dot_general | solution.py:35
  496.4 15.0 %convert_bitcast_fusion = bf16[8,8,48,2048]{3,2,0,1:T(8,128)(2,1)} fusion(bf16[8,352,2048]{2,1,0:T(8,128)(2,1)} %param.15, f32[8,8,48,2,352]{4,2,3,0,1:T(8,128)} %fusion.12), kind=kOutput, calls=%fused_computation.7 | convolution fusion | flops 4441964544 | bytes 32768000 | tf_op jit(solution)/shard_map/aenf,efd->aend/dot_general | solution.py:37
  511.4 10.8 %copy.114 = bf16[8,8,48,2048]{3,2,1,0:T(8,128)(2,1)} copy(bf16[8,8,48,2048]{3,2,0,1:T(8,128)(2,1)} %convert_bitcast_fusion) | data formatting | bytes 25165824 | tf_op jit(solution)/shard_map/convert_element_type | solution.py:108
  522.2 5.5 all-to-all-start.3
  527.7 0.3 reduce-scatter.2.cloned.1.call-start
  528.0 0.2 sub.33
  528.2 0.1 compare_select_fusion
  528.3 0.1 reshape.223
  528.5 0.6 fusion.39
  529.3 0.1 copy.105
  529.4 272.1 %all-to-all-done.3 = bf16[8,8,48,2048]{3,2,1,0:T(8,128)(2,1)} async-done(((bf16[8,8,48,2048]{3,2,1,0:T(8,128)(2,1)}), bf16[8,8,48,2048]{3,2,1,0:T(8,128)(2,1)}, u32[]{:S(2)}, u32[]{:S(2)}) %all-to-all-start.3) | async-done | bytes 12582944 | tf_op jit(solution)/shard_map/all_to_all | solution.py:109
  801.5 24.5 %gather_fusion = bf16[2304,2048]{1,0:T(8,128)(2,1)} fusion(bf16[3072,2048]{1,0:T(8,128)(2,1)} %bitcast.24, s32[3072]{0:T(1024)S(1)} %pad_clamp_fusion), kind=kCustom, calls=%fused_computation | custom fusion | bytes 18883584 | tf_op jit(solution)/shard_map/gather | solution.py:50
  826.0 16.9 %reshape.238 = f32[384,6,2048]{2,1,0:T(8,128)} reshape(bf16[2304,2048]{1,0:T(8,128)(2,1)} %gather_fusion) | data formatting | bytes 28311552 | tf_op jit(solution)/shard_map/convert_element_type | solution.py:50
  842.8 14.5 %multiply_reduce_fusion = bf16[384,2048]{1,0:T(8,128)(2,1)} fusion(f32[384,6,2048]{2,1,0:T(8,128)} %reshape.238, f32[384,6]{1,0:T(8,128)S(1)} %copy.105), kind=kLoop, calls=%fused_computation.3 | loop fusion | flops 8650752 | bytes 20456448 | tf_op jit(solution)/shard_map/reduce_sum | solution.py:51
  857.4 29.0 %reduce-scatter.2.cloned.1.call-done = bf16[96,2048]{1,0:T(8,128)(2,1)} async-done(((bf16[384,2048]{1,0:T(8,128)(2,1)}), bf16[96,2048]{1,0:T(8,128)(2,1)}) %reduce-scatter.2.cloned.1.call-update) | async-done | bytes 393232 | tf_op jit(solution)/shard_map/reduce_scatter | solution.py:111
  886.3 1.8 fusion.24
  (36 shorter events, 1.1 us)
Async XLA Ops:
  6.5 522.0 %copy-start = (bf16[2048,64]{0,1:T(8,128)(2,1)S(1)}, bf16[2048,64]{0,1:T(8,128)(2,1)}, u32[]{:S(2)}) copy-start(bf16[2048,64]{0,1:T(8,128)(2,1)} %param.12) | copy-start | bytes 786436
  6.5 102.8 %all-gather.3.cloned.1.call-start = ((), (), s32[]{:S(2)}) async-start(), calls=%async_computation.5 | async-start | bytes 10485760 | tf_op jit(solution)/shard_map/all_gather | solution.py:89
  7.3 139.1 %all-gather.5.cloned.1.call-start = ((), (), s32[]{:S(2)}) async-start(), calls=%async_computation.6 | async-start | bytes 1966080 | tf_op jit(solution)/shard_map/all_gather | solution.py:97
  37.5 71.9 %copy-start.2 = (bf16[1,96,2048]{2,1,0:T(8,128)(2,1)S(1)}, bf16[1,96,2048]{2,1,0:T(8,128)(2,1)}, u32[]{:S(2)}) copy-start(bf16[1,96,2048]{2,1,0:T(8,128)(2,1)} %param.8) | copy-start | bytes 1179652
  57.0 57.4 %copy-start.4 = (f32[2048]{0:T(1024)S(1)}, f32[2048]{0:T(1024)}, u32[]{:S(2)}) copy-start(f32[2048]{0:T(1024)} %param.11) | copy-start | bytes 24580
  57.4 57.9 %copy-start.3 = (s32[1,384,6]{1,0,2:T(1,128)S(1)}, s32[1,384,6]{1,0,2:T(1,128)}, u32[]{:S(2)}) copy-start(s32[1,384,6]{1,0,2:T(1,128)} %param.13) | copy-start | bytes 27652
  522.2 6.3 copy-start.1
  522.2 279.3 %all-to-all-start.3 = ((bf16[8,8,48,2048]{3,2,1,0:T(8,128)(2,1)}), bf16[8,8,48,2048]{3,2,1,0:T(8,128)(2,1)}, u32[]{:S(2)}, u32[]{:S(2)}) async-start(bf16[8,8,48,2048]{3,2,1,0:T(8,128)(2,1)} %copy.114), calls=%async_computation.3 | async-start | bytes 25165824 | tf_op jit(solution)/shard_map/all_to_all | solution.py:109
  527.7 358.6 %reduce-scatter.2.cloned.1.call-start = ((), (), s32[]{:S(2)}) async-start(), calls=%async_computation.7 | async-start | bytes 1966080 | tf_op jit(solution)/shard_map/reduce_scatter | solution.py:111
Sparse Core Ops, SparseCore 0:
  9.2 100.1 all-gather.2
  115.4 30.9 all-gather.4
  857.5 28.7 reduce-scatter.1
where the time goes:
time: 896 us; the launch traced here: 895 us
  waiting for transfers between devices  377 us (42%)
  blocking collectives  321 us (36%)
  local copies, waits for them, and re-layouts  105 us (12%)
  matrix products  47.3 us (5%)
  other arithmetic  24.9 us (3%)
  between operations  13.4 us (1%)
    all_to_all x1, blocking collectives, on_device(): lax.all_to_all(outgoing, 'exp', split_axis=0, concat_axis=0, tiled=True)  281 us
    all_to_all x1, waiting for transfers between devices, on_device(): lax.all_to_all(partial_out, 'exp', split_axis=0, concat_axis=0, tiled=True)  272 us
    all_gather x1, waiting for transfers between devices, on_device(): lax.all_gather(w_out, 'seq', axis=0, tiled=True)  51.9 us
    reduce_scatter x1, waiting for transfers between devices, on_device(): lax.psum_scatter(combine_rows(out_table, slot_index, gate_vals).astype(jn...  29 us
    all_to_all x1, blocking collectives, on_device(): lax.all_to_all(packed, 'seq', split_axis=2, concat_axis=0, tiled=True)  27.1 us
    gather x1, local copies, waits for them, and re-layouts, combine_rows(): picked = out_table[slot_index].astype(jnp.float32)  24.5 us
    scatter x1, local copies, waits for them, and re-layouts, scatter_rows(): empty.at[slot_index.reshape(-1)].set(spread.reshape(-1, feature_width))  23.8 us
    all_gather x1, waiting for transfers between devices, on_device(): gathered = lax.all_gather(normed, 'seq', axis=0, tiled=True)  23.2 us
  transfers between devices with their start and end apart: 4, of which 4 were waited for; matrix products, arithmetic and copies ran while one was open for 2% of the time, Pallas kernels for 0%

commit v1 on v0

v1 whole, which is shorter than its diff:
```python
import math

import jax
import jax.numpy as jnp
from jax import lax
from jax.sharding import PartitionSpec as P

H = 16
HD = 128

epsilon = 1e-05


def gate_table(normed_rows, router_w, chosen):
    logits = jnp.dot(normed_rows, router_w, preferred_element_type=jnp.float32)
    experts = jnp.arange(logits.shape[1], dtype=jnp.int32)
    picked = jnp.any(chosen[:, :, None] == experts[None, None, :], axis=1)
    squashed = jnp.where(picked, jax.nn.sigmoid(logits), 0.0)
    gates = squashed / jnp.sum(squashed, axis=-1, keepdims=True)
    return jnp.where(picked, gates, -1.0)


def on_device(resid, qkv, w_out, norm_gain, router_w, expert_ids, w_gate_up, w_down):
    rows = resid.shape[1]
    width = resid.shape[2]
    seq_size = lax.axis_size("seq")
    exp_size = lax.axis_size("exp")
    set_rows = rows * seq_size
    head_local = H // seq_size
    local_width = head_local * HD
    blocks = seq_size * exp_size
    exp_local = w_gate_up.shape[0]
    experts = router_w.shape[1]
    cap = rows // 8

    packed = qkv.reshape(rows, 3, seq_size, local_width)
    regrouped = lax.all_to_all(packed, "seq", split_axis=2, concat_axis=0, tiled=True)
    q = regrouped[:, 0, 0].reshape(set_rows, head_local, HD)
    k = regrouped[:, 1, 0].reshape(set_rows, head_local, HD)
    v = regrouped[:, 2, 0].reshape(set_rows, head_local, HD)
    scores = jnp.einsum("qhd,khd->hqk", q, k, preferred_element_type=jnp.float32) / math.sqrt(HD)
    probs = jax.nn.softmax(scores, axis=-1).astype(jnp.bfloat16)
    attended = jnp.einsum("hqk,khd->qhd", probs, v, preferred_element_type=jnp.float32)
    attended = attended.astype(jnp.bfloat16).reshape(set_rows, local_width)
    part = jnp.dot(attended, w_out, preferred_element_type=jnp.float32).astype(jnp.bfloat16)
    projected = lax.psum_scatter(part, "seq", scatter_dimension=0, tiled=True)
    mixed = resid[0].astype(jnp.float32) + projected.astype(jnp.float32)
    meansq = jnp.mean(mixed * mixed, axis=-1, keepdims=True)
    normed = (mixed * lax.rsqrt(meansq + epsilon) * norm_gain).astype(jnp.bfloat16)

    chosen = lax.dynamic_slice_in_dim(expert_ids[0], lax.axis_index("seq") * rows, rows, 0)
    gates = gate_table(normed, router_w, chosen)
    high = gates.astype(jnp.bfloat16)
    low = (gates - high.astype(jnp.float32)).astype(jnp.bfloat16)
    sent = jnp.concatenate([normed, high, low], axis=1)
    everyone = lax.all_gather(sent, ("exp", "seq"), axis=0, tiled=True)
    points = everyone[:, :width].reshape(blocks, rows, width)
    first = lax.axis_index("exp") * exp_local
    high = lax.dynamic_slice_in_dim(everyone[:, width : width + experts], first, exp_local, 1)
    low = lax.dynamic_slice_in_dim(everyone[:, width + experts :], first, exp_local, 1)
    gates = (high.astype(jnp.float32) + low.astype(jnp.float32)).reshape(blocks, rows, exp_local)
    named = high.reshape(blocks, rows, exp_local) >= 0
    before = jnp.tril(jnp.ones((rows, rows), jnp.bfloat16), -1)
    ranks = jnp.einsum(
        "rs,bse->ber", before, named.astype(jnp.bfloat16), preferred_element_type=jnp.float32
    ).astype(jnp.int32)
    place = named.transpose(0, 2, 1)[:, :, None, :] & (
        ranks[:, :, None, :] == jnp.arange(cap, dtype=jnp.int32)[None, None, :, None]
    )
    slot_gate = jnp.sum(jnp.where(place, gates.transpose(0, 2, 1)[:, :, None, :], 0.0), axis=-1)
    place = place.astype(jnp.bfloat16).reshape(blocks, exp_local * cap, rows)
    slots = jnp.einsum("bsr,brd->bsd", place, points, preferred_element_type=jnp.float32)
    slots = slots.astype(jnp.bfloat16).reshape(blocks, exp_local, cap, width)
    both = jnp.einsum("bend,edgf->bengf", slots, w_gate_up, preferred_element_type=jnp.float32)
    hidden = (jax.nn.silu(both[:, :, :, 0]) * both[:, :, :, 1]).astype(jnp.bfloat16)
    outs = jnp.einsum("benf,efd->bend", hidden, w_down, preferred_element_type=jnp.float32)
    outs = (outs * slot_gate[..., None]).astype(jnp.bfloat16).reshape(blocks, -1, width)
    sums = jnp.einsum("bsr,bsd->brd", place, outs, preferred_element_type=jnp.float32)
    sums = sums.astype(jnp.bfloat16).reshape(blocks * rows, width)
    expert_sum = lax.psum_scatter(sums, ("exp", "seq"), scatter_dimension=0, tiled=True)
    out = mixed + expert_sum.astype(jnp.float32)
    return out.astype(jnp.bfloat16).reshape(1, rows, width)


def solution(mesh):
    in_specs = (
        P("exp", "seq", None),
        P("exp", "seq", None),
        P("seq", None),
        P(),
        P(),
        P("exp", None, None),
        P("exp", None, None, "seq"),
        P("exp", "seq", None),
    )
    return jax.shard_map(
        on_device,
        mesh=mesh,
        in_specs=in_specs,
        out_specs=P("exp", "seq", None),
        check_vma=False,
    )
```

time: 896 us -> 446 us (0.50)
  blocking collectives: 321 us -> 20.5 us
  waiting for transfers between devices: 377 us -> 283 us
  local copies, waits for them, and re-layouts: 105 us -> 37.7 us
  matrix products: 47.3 us -> 83.6 us
  other arithmetic: 24.9 us -> 7.26 us
    all_to_all x2 -> x0, blocking collectives: 294 us -> none  [the longest x1 281 us: on_device(): lax.all_to_all(outgoing, 'exp', split_axis=0, concat_axis=0, tiled=True)]
    all_to_all x1 -> x0, waiting for transfers between devices: 272 us -> none  [on_device(): lax.all_to_all(partial_out, 'exp', split_axis=0, concat_axis=0, tiled=True)]
    reduce_scatter x1 -> x2, waiting for transfers between devices: 29 us -> 184 us  [the longest x1 154 us: on_device(): lax.psum_scatter(sums, ('exp', 'seq'), scatter_dimension=0, tiled=True)]
    dot_general x5 -> x8, matrix products: 45 us -> 80.4 us  [the longest x1 25.2 us: on_device(): jnp.einsum('bsr,bsd->brd', place, outs, preferred_element_type=jnp.float32)]
    gather x1 -> x0, local copies, waits for them, and re-layouts: 24.5 us -> none  [combine_rows(): picked = out_table[slot_index].astype(jnp.float32)]
    all_gather x2 -> x1, waiting for transfers between devices: 75.1 us -> 99.6 us  [on_device(): everyone = lax.all_gather(sent, ('exp', 'seq'), axis=0, tiled=True)]
    scatter x1 -> x0, local copies, waits for them, and re-layouts: 23.8 us -> none  [scatter_rows(): empty.at[slot_index.reshape(-1)].set(spread.reshape(-1, feature_width))]
    reshape x3 -> x2, local copies, waits for them, and re-layouts: 18 us -> 2.35 us  [on_device(): packed = qkv.reshape(rows, 3, seq_size, local_width)]
  transfers between devices with their start and end apart: 4 -> 3, of which waited for: 4 -> 3; matrix products, arithmetic and copies ran while one was open for 2% -> 0% of each run, Pallas kernels for 0% -> 0%
where the time goes in v1:
time: 446 us
  waiting for transfers between devices  283 us (63%)
  matrix products  83.6 us (19%)
  local copies, waits for them, and re-layouts  37.7 us (8%)
  blocking collectives  20.5 us (5%)
  between operations  13.3 us (3%)
  other arithmetic  7.26 us (2%)
    reduce_scatter x1, waiting for transfers between devices, on_device(): lax.psum_scatter(sums, ('exp', 'seq'), scatter_dimension=0, tiled=True)  154 us
    all_gather x1, waiting for transfers between devices, on_device(): everyone = lax.all_gather(sent, ('exp', 'seq'), axis=0, tiled=True)  99.6 us
    reduce_scatter x1, waiting for transfers between devices, on_device(): projected = lax.psum_scatter(part, 'seq', scatter_dimension=0, tiled=True)  29.8 us
    dot_general x1, matrix products, on_device(): jnp.einsum('bsr,bsd->brd', place, outs, preferred_element_type=jnp.float32)  25.2 us
    dot_general x1, matrix products, on_device(): jnp.einsum('bend,edgf->bengf', slots, w_gate_up, preferred_element_type=j...  22.3 us
    all_to_all x1, blocking collectives, on_device(): lax.all_to_all(packed, 'seq', split_axis=2, concat_axis=0, tiled=True)  20.5 us
    dot_general x1, matrix products, on_device(): jnp.einsum('benf,efd->bend', hidden, w_down, preferred_element_type=jnp.f...  15.4 us
    convert_element_type x1, local copies, waits for them, and re-layouts, on_device(): slots = slots.astype(jnp.bfloat16).reshape(blocks, exp_local, cap, width)  14.5 us
  transfers between devices with their start and end apart: 3, of which 3 were waited for; matrix products, arithmetic and copies ran while one was open for 0% of the time, Pallas kernels for 0%

profile of v1, /device:TPU:0, one launch (start us, length us, event | category | flops | bytes accessed | tf_op | source)
XLA Modules:
  0.0 445.7 jit_solution(5018050210532123831)
XLA Ops:
  6.5 2.1 reshape.52
  8.7 0.2 copy.91
  8.9 20.5 %all_to_all.18 = bf16[96,3,4,512]{3,0,1,2:T(8,128)(2,1)S(1)} all-to-all(bf16[96,3,4,512]{3,0,1,2:T(8,128)(2,1)S(1)} %copy.91), channel_id=1, replica_groups=mesh['seq'=4,'exp'=8] {'seq'}, dimensions={2} | all-to-all | bytes 2359296 | tf_op jit(solution)/shard_map/all_to_all | solution.py:37
  29.4 0.1 copy.92
  29.5 0.1 fusion.46
  29.6 0.9 copy.97
  30.5 0.9 copy.93
  31.4 0.2 copy.94
  31.6 3.3 fusion.47
  34.9 2.1 convolution_convert_fusion.2
  37.0 0.0 copy-start.2
  37.0 0.0 copy-start.5
  37.0 0.0 copy-start.6
  37.1 2.2 convolution_convert_fusion.1
  39.2 0.0 reduce-scatter.3.cloned.1.call-update
  39.2 0.0 all-gather.2.cloned.1.call-start
  39.3 0.8 constant_dynamic-slice_fusion
  40.1 0.1 copy.102
  40.2 29.8 %reduce-scatter.3.cloned.1.call-done = bf16[96,2048]{1,0:T(8,128)(2,1)} async-done(((bf16[384,2048]{1,0:T(8,128)(2,1)}), bf16[96,2048]{1,0:T(8,128)(2,1)}) %reduce-scatter.3.cloned.1.call-update) | async-done | bytes 393232 | tf_op jit(solution)/shard_map/reduce_scatter | solution.py:46
  70.1 1.2 multiply_reduce_fusion.1
  71.3 1.2 multiply_convert_fusion
  72.5 0.0 copy-done.6
  72.5 0.4 fusion.48
  72.8 0.1 subtract_convert_fusion
  72.9 0.9 concatenate.3
  73.8 0.0 all-gather.2.cloned.1.call-update
  73.8 0.0 reduce-scatter.5.cloned.1.call-start
  73.9 0.1 eq.46
  74.0 99.6 %all-gather.2.cloned.1.call-done = bf16[3072,2176]{1,0:T(8,128)(2,1)} async-done(((bf16[96,2176]{1,0:T(8,128)(2,1)}), bf16[3072,2176]{1,0:T(8,128)(2,1)}) %all-gather.2.cloned.1.call-update) | async-done | bytes 13369360 | tf_op jit(solution)/shard_map/all_gather | solution.py:56
  173.5 1.9 fusion.45
  175.5 0.4 dynamic-slice_compare_fusion
  175.9 0.5 copy.104
  176.3 0.5 copy.103
  176.8 0.2 convolution_convert_fusion.3
  177.0 0.3 fusion.24
  177.4 1.1 copy.109
  178.5 1.6 convert_add_fusion
  180.2 1.9 copy.108
  182.0 0.5 select_reduce_fusion
  182.5 10.9 %slice.36 = bf16[3072,2048]{1,0:T(8,128)(2,1)} slice(bf16[3072,2176]{1,0:T(8,128)(2,1)} %all-gather.2.cloned.1.call-done), slice={[0:3072], [0:2048]} | slice | bytes 25165824 | tf_op jit(solution)/shard_map/slice | solution.py:57
  193.5 12.6 %convolution_convert_fusion = bf16[32,96,2048]{2,1,0:T(8,128)(2,1)} fusion(pred[32,96,96]{1,2,0:T(32,128)(4,1)S(1)} %copy.109, bf16[32,96,2048]{2,1,0:T(8,128)(2,1)} %bitcast.92), kind=kOutput, calls=%fused_computation.10 | convolution fusion | flops 1214251008 | bytes 25460736 | tf_op jit(solution)/shard_map/bsr,brd->bsd/dot_general | solution.py:72
  206.1 14.5 %copy.106 = bf16[32,96,2048]{2,0,1:T(8,128)(2,1)} copy(bf16[32,96,2048]{2,1,0:T(8,128)(2,1)} %convolution_convert_fusion) | data formatting | bytes 25165824 | tf_op jit(solution)/shard_map/convert_element_type | solution.py:73
  220.6 22.3 %fusion.15 = f32[32,8,12,2,352]{4,0,3,2,1:T(8,128)} fusion(bf16[32,8,12,2048,1]{3,0,4,2,1:T(8,128)(2,1)} %bitcast.95, bf16[8,2048,2,352]{1,3,2,0:T(8,128)(2,1)} %param.14), kind=kOutput, calls=%fused_computation.15 | convolution fusion | flops 8858370048 | bytes 44302336 | tf_op jit(solution)/shard_map/bend,edgf->bengf/dot_general | solution.py:74
  242.9 15.4 %fusion.1 = bf16[32,8,12,2048]{3,0,2,1:T(8,128)(2,1)} fusion(f32[32,8,12]{0,2,1:T(8,128)S(1)} %select_reduce_fusion, bf16[8,352,2048]{2,1,0:T(8,128)(2,1)} %param.15, f32[32,8,12,2,352]{4,0,3,2,1:T(8,128)} %fusion.15), kind=kOutput, calls=%fused_computation.2 | convolution fusion | flops 4448256000 | bytes 32780288 | tf_op jit(solution)/shard_map/benf,efd->bend/dot_general | solution.py:76
  258.3 25.2 %fusion.10 = bf16[32,96,2048]{2,1,0:T(8,128)(2,1)} fusion(pred[32,96,96]{1,2,0:T(32,128)(4,1)S(1)} %copy.109, bf16[32,96,2048]{2,0,1:T(8,128)(2,1)} %bitcast.94), kind=kOutput, calls=%fused_computation.9 | convolution fusion | flops 1214251008 | bytes 25460736 | tf_op jit(solution)/shard_map/bsr,bsd->brd/dot_general | solution.py:78
  283.5 0.0 reduce-scatter.5.cloned.1.call-update
  283.5 153.7 %reduce-scatter.5.cloned.1.call-done = bf16[96,2048]{1,0:T(8,128)(2,1)} async-done(((bf16[3072,2048]{1,0:T(8,128)(2,1)}), bf16[96,2048]{1,0:T(8,128)(2,1)}) %reduce-scatter.5.cloned.1.call-update) | async-done | bytes 393232 | tf_op jit(solution)/shard_map/reduce_scatter | solution.py:80
  437.3 1.9 fusion.30
  (16 shorter events, 0.1 us)
Async XLA Ops:
  6.5 30.5 %copy-start = (bf16[512,2048]{1,0:T(8,128)(2,1)S(1)}, bf16[512,2048]{1,0:T(8,128)(2,1)}, u32[]{:S(2)}) copy-start(bf16[512,2048]{1,0:T(8,128)(2,1)} %param.10) | copy-start | bytes 6291460
  6.5 63.5 %reduce-scatter.3.cloned.1.call-start = ((), (), s32[]{:S(2)}) async-start(), calls=%async_computation.3 | async-start | bytes 1966080 | tf_op jit(solution)/shard_map/reduce_scatter | solution.py:46
  30.5 4.4 copy-start.4
  37.0 33.1 %copy-start.2 = (bf16[1,96,2048]{2,1,0:T(8,128)(2,1)S(1)}, bf16[1,96,2048]{2,1,0:T(8,128)(2,1)}, u32[]{:S(2)}) copy-start(bf16[1,96,2048]{2,1,0:T(8,128)(2,1)} %param.8) | copy-start | bytes 1179652
  37.0 34.3 %copy-start.5 = (f32[2048]{0:T(1024)S(1)}, f32[2048]{0:T(1024)}, u32[]{:S(2)}) copy-start(f32[2048]{0:T(1024)} %param.11) | copy-start | bytes 24580
  37.0 35.4 %copy-start.6 = (bf16[2048,64]{0,1:T(8,128)(2,1)S(1)}, bf16[2048,64]{0,1:T(8,128)(2,1)}, u32[]{:S(2)}) copy-start(bf16[2048,64]{0,1:T(8,128)(2,1)} %param.12) | copy-start | bytes 786436
  39.2 134.3 %all-gather.2.cloned.1.call-start = ((), (), s32[]{:S(2)}) async-start(), calls=%async_computation.4 | async-start | bytes 13787136 | tf_op jit(solution)/shard_map/all_gather | solution.py:56
  73.8 363.4 %reduce-scatter.5.cloned.1.call-start = ((), (), s32[]{:S(2)}) async-start(), calls=%async_computation.5 | async-start | bytes 12976128 | tf_op jit(solution)/shard_map/reduce_scatter | solution.py:80
  283.5 155.6 %copy-start.1 = (bf16[512,2048]{1,0:T(8,128)(2,1)S(1)}, bf16[512,2048]{1,0:T(8,128)(2,1)}, u32[]{:S(2)}) copy-start(bf16[512,2048]{1,0:T(8,128)(2,1)} %param.10) | copy-start | bytes 6291460
  283.5 153.7 %copy-start.3 = (bf16[96,2048]{1,0:T(8,128)(2,1)S(1)}, bf16[96,2048]{1,0:T(8,128)(2,1)}, u32[]{:S(2)}) copy-start(bf16[96,2048]{1,0:T(8,128)(2,1)} %reduce-scatter.3.cloned.1.call-done) | copy-start | bytes 1179652
Sparse Core Ops, SparseCore 0:
  39.4 30.6 reduce-scatter.2
  73.9 99.5 all-gather.1
  283.7 153.5 reduce-scatter.4

commit v2 on v1

--- a/solution.py
+++ b/solution.py
@@ -1,8 +1,11 @@
+import functools
 import math
 
 import jax
 import jax.numpy as jnp
 from jax import lax
+from jax.experimental import pallas as pl
+from jax.experimental.pallas import tpu as pltpu
 from jax.sharding import PartitionSpec as P
 
 H = 16
@@ -18,6 +21,163 @@
     squashed = jnp.where(picked, jax.nn.sigmoid(logits), 0.0)
     gates = squashed / jnp.sum(squashed, axis=-1, keepdims=True)
     return jnp.where(picked, gates, -1.0)
+
+
+MESH = pl.DeviceIdType.MESH
+
+
+def greet(chips, seq_size):
+    exp, seq = lax.axis_index("exp"), lax.axis_index("seq")
+    chip, core = exp // 2, exp % 2
+    barrier = pltpu.get_barrier_semaphore()
+    pl.semaphore_signal(
+        barrier, inc=1, device_id={"exp": chip * 2 + 1 - core, "seq": seq}, device_id_type=MESH
+    )
+    for j in range(1, seq_size):
+        pl.semaphore_signal(
+            barrier,
+            inc=1,
+            device_id={"exp": exp, "seq": (seq + j) % seq_size},
+            device_id_type=MESH,
+        )
+    for i in range(1, chips):
+        pl.semaphore_signal(
+            barrier,
+            inc=1,
+            device_id={"exp": (chip + i) % chips * 2 + core, "seq": seq},
+            device_id_type=MESH,
+        )
+    pl.semaphore_wait(barrier, seq_size + chips - 1)
+
+
+def scatter_kernel(
+    chips, seq_size, x_ref, out_ref, pair, by_seq, done, by_chip, s0, r0, s1, r1, s2, r2
+):
+    exp, seq = lax.axis_index("exp"), lax.axis_index("seq")
+    chip, core = exp // 2, exp % 2
+    rows = out_ref.shape[0]
+    step = 16
+    parts = rows // step
+    greet(chips, seq_size)
+
+    def target(i):
+        return (chip + 1 + i) % chips
+
+    def copy(src, dst, send, recv, e, s):
+        made = pltpu.make_async_remote_copy(
+            src_ref=src,
+            dst_ref=dst,
+            send_sem=send,
+            recv_sem=recv,
+            device_id={"exp": e, "seq": s},
+            device_id_type=MESH,
+        )
+        made.start()
+        return made
+
+    to_core = [
+        copy(
+            x_ref.at[target(i) * 2 + 1 - core],
+            pair.at[i],
+            s0.at[i],
+            r0.at[i],
+            chip * 2 + 1 - core,
+            seq,
+        )
+        for i in range(chips)
+    ]
+    to_seq, to_chip = [], []
+
+    def finish(i):
+        for c in to_seq[i]:
+            c.wait_recv()
+        last = i == chips - 1
+
+        @pl.loop(0, parts)
+        def _(t):
+            at = pl.ds(pl.multiple_of(t * step, step), step)
+            total = pair[i, seq, at, :].astype(jnp.float32)
+            for j in range(seq_size - 1):
+                total += by_seq[j, i, at, :].astype(jnp.float32)
+            if last:
+                out_ref[at, :] = total
+            else:
+                done[i, at, :] = total.astype(jnp.bfloat16)
+
+        if not last:
+            to_chip.append(
+                copy(
+                    done.at[i], by_chip.at[i], s2.at[i], r2.at[i], target(i) * 2 + core, seq
+                )
+            )
+
+    for i in range(chips):
+        to_core[i].wait_recv()
+
+        @pl.loop(0, seq_size * parts)
+        def _(t):
+            p = t // parts
+            at = pl.ds(pl.multiple_of(t % parts * step, step), step)
+            mine = x_ref[target(i) * 2 + core, p, at, :].astype(jnp.float32)
+            pair[i, p, at, :] = (mine + pair[i, p, at, :].astype(jnp.float32)).astype(jnp.bfloat16)
+
+        sends = []
+        for j in range(1, seq_size):
+            peer = (seq + j) % seq_size
+            sends.append(
+                copy(
+                    pair.at[i, peer],
+                    by_seq.at[j - 1, i],
+                    s1.at[i, j - 1],
+                    r1.at[i, j - 1],
+                    exp,
+                    peer,
+                )
+            )
+        to_seq.append(sends)
+        if i > 0:
+            finish(i - 1)
+    finish(chips - 1)
+    for c in to_chip:
+        c.wait_recv()
+
+    @pl.loop(0, parts)
+    def _(t):
+        at = pl.ds(pl.multiple_of(t * step, step), step)
+        total = out_ref[at, :]
+        for i in range(chips - 1):
+            total += by_chip[i, at, :].astype(jnp.float32)
+        out_ref[at, :] = total
+
+    for c in to_core + [c for sends in to_seq for c in sends] + to_chip:
+        c.wait_send()
+
+
+def reduce_blocks(sums, exp_size, seq_size):
+    rows, width = sums.shape[2:]
+    chips = exp_size // 2
+    dma = pltpu.SemaphoreType.DMA
+    return pl.pallas_call(
+        functools.partial(scatter_kernel, chips, seq_size),
+        out_shape=jax.ShapeDtypeStruct((rows, width), jnp.float32),
+        in_specs=[pl.BlockSpec(memory_space=pltpu.VMEM)],
+        out_specs=pl.BlockSpec(memory_space=pltpu.VMEM),
+        scratch_shapes=[
+            pltpu.VMEM((chips, seq_size, rows, width), jnp.bfloat16),
+            pltpu.VMEM((seq_size - 1, chips, rows, width), jnp.bfloat16),
+            pltpu.VMEM((chips - 1, rows, width), jnp.bfloat16),
+            pltpu.VMEM((chips - 1, rows, width), jnp.bfloat16),
+            dma((chips,)),
+            dma((chips,)),
+            dma((chips, seq_size - 1)),
+            dma((chips, seq_size - 1)),
+            dma((chips - 1,)),
+            dma((chips - 1,)),
+        ],
+        compiler_params=pltpu.CompilerParams(
+            collective_id=0, has_side_effects=True, vmem_limit_bytes=48 << 20
+        ),
+    )(sums)
 
 
 def on_device(resid, qkv, w_out, norm_gain, router_w, expert_ids, w_gate_up, w_down):
@@ -77,7 +237,12 @@
     outs = (outs * slot_gate[..., None]).astype(jnp.bfloat16).reshape(blocks, -1, width)
     sums = jnp.einsum("bsr,bsd->brd", place, outs, preferred_element_type=jnp.float32)
     sums = sums.astype(jnp.bfloat16).reshape(blocks * rows, width)
-    expert_sum = lax.psum_scatter(sums, ("exp", "seq"), scatter_dimension=0, tiled=True)
+    if exp_size > 8:
+        expert_sum = lax.psum_scatter(sums, ("exp", "seq"), scatter_dimension=0, tiled=True)
+    else:
+        expert_sum = reduce_blocks(
+            sums.reshape(exp_size, seq_size, rows, width), exp_size, seq_size
+        )
     out = mixed + expert_sum.astype(jnp.float32)
     return out.astype(jnp.bfloat16).reshape(1, rows, width)
 

time: 446 us -> 373 us (0.84)
  waiting for transfers between devices: 283 us -> 129 us
  Pallas kernels: 0 us -> 81 us
    reduce_scatter x1 -> x0, waiting for transfers between devices: 154 us -> none  [on_device(): lax.psum_scatter(sums, ('exp', 'seq'), scatter_dimension=0, tiled=True)]
    pallas_call x0 -> x1, Pallas kernels: none -> 81 us  [reduce_blocks(): pl.pallas_call(functools.partial(scatter_kernel, chips, seq_size), out_sh...]
  transfers between devices with their start and end apart: 3 -> 2, of which waited for: 3 -> 2; matrix products, arithmetic and copies ran while one was open for 0% -> 0% of each run, Pallas kernels for 0% -> 0%
where the time goes in v2:
time: 373 us; the launch traced here: 372 us
  waiting for transfers between devices  129 us (35%)
  matrix products  83.6 us (22%)
  Pallas kernels  81 us (22%)
  local copies, waits for them, and re-layouts  37.7 us (10%)
  blocking collectives  20.5 us (5%)
  between operations  13.6 us (4%)
  other arithmetic  6.24 us (2%)
    all_gather x1, waiting for transfers between devices, on_device(): everyone = lax.all_gather(sent, ('exp', 'seq'), axis=0, tiled=True)  99.6 us
    pallas_call x1, Pallas kernels, reduce_blocks(): pl.pallas_call(functools.partial(scatter_kernel, chips, seq_size), out_sh...  81 us
    reduce_scatter x1, waiting for transfers between devices, on_device(): projected = lax.psum_scatter(part, 'seq', scatter_dimension=0, tiled=True)  29.8 us
    dot_general x1, matrix products, on_device(): jnp.einsum('bsr,bsd->brd', place, outs, preferred_element_type=jnp.float32)  25.2 us
    dot_general x1, matrix products, on_device(): jnp.einsum('bend,edgf->bengf', slots, w_gate_up, preferred_element_type=j...  22.3 us
    all_to_all x1, blocking collectives, on_device(): lax.all_to_all(packed, 'seq', split_axis=2, concat_axis=0, tiled=True)  20.5 us
    dot_general x1, matrix products, on_device(): jnp.einsum('benf,efd->bend', hidden, w_down, preferred_element_type=jnp.f...  15.4 us
    convert_element_type x1, local copies, waits for them, and re-layouts, on_device(): slots = slots.astype(jnp.bfloat16).reshape(blocks, exp_local, cap, width)  14.5 us
  transfers between devices with their start and end apart: 2, of which 2 were waited for; matrix products, arithmetic and copies ran while one was open for 0% of the time, Pallas kernels for 0%

profile of v2, /device:TPU:0, one launch (start us, length us, event | category | flops | bytes accessed | tf_op | source)
XLA Modules:
  0.0 372.2 jit_solution(4357235531166827441)
XLA Ops:
  6.5 0.0 copy-start
  6.5 2.1 reshape.49
  8.7 0.2 copy.91
  8.9 20.5 %all_to_all.18 = bf16[96,3,4,512]{3,0,1,2:T(8,128)(2,1)S(1)} all-to-all(bf16[96,3,4,512]{3,0,1,2:T(8,128)(2,1)S(1)} %copy.91), channel_id=1, replica_groups=mesh['seq'=4,'exp'=8] {'seq'}, dimensions={2} | all-to-all | bytes 2359296 | tf_op jit(solution)/shard_map/all_to_all | solution.py:197
  29.4 0.1 copy.92
  29.5 0.1 fusion.46
  29.6 0.9 copy.97
  30.5 0.9 copy.93
  31.4 0.2 copy.94
  31.6 3.3 fusion.47
  34.9 2.1 convolution_convert_fusion.2
  37.0 0.0 copy-start.2
  37.0 0.0 copy-start.5
  37.0 0.0 copy-start.6
  37.1 2.2 convolution_convert_fusion.1
  39.2 0.0 reduce-scatter.2.cloned.1.call-update
  39.2 0.0 all-gather.2.cloned.1.call-start
  39.3 0.8 constant_dynamic-slice_fusion
  40.1 0.1 copy.102
  40.2 29.8 %reduce-scatter.2.cloned.1.call-done = bf16[96,2048]{1,0:T(8,128)(2,1)} async-done(((bf16[384,2048]{1,0:T(8,128)(2,1)}), bf16[96,2048]{1,0:T(8,128)(2,1)}) %reduce-scatter.2.cloned.1.call-update) | async-done | bytes 393232 | tf_op jit(solution)/shard_map/reduce_scatter | solution.py:206
  70.1 1.2 multiply_reduce_fusion.1
  71.3 1.2 multiply_convert_fusion
  72.5 0.0 copy-done.6
  72.5 0.4 fusion.48
  72.8 0.1 subtract_convert_fusion
  72.9 0.9 concatenate.3
  73.8 0.0 all-gather.2.cloned.1.call-update
  73.8 0.1 eq.46
  73.9 99.6 %all-gather.2.cloned.1.call-done = bf16[3072,2176]{1,0:T(8,128)(2,1)} async-done(((bf16[96,2176]{1,0:T(8,128)(2,1)}), bf16[3072,2176]{1,0:T(8,128)(2,1)}) %all-gather.2.cloned.1.call-update) | async-done | bytes 13369360 | tf_op jit(solution)/shard_map/all_gather | solution.py:216
  173.5 1.9 fusion.45
  175.5 0.4 dynamic-slice_compare_fusion
  175.9 0.5 copy.104
  176.3 0.5 copy.103
  176.8 0.2 convolution_convert_fusion.3
  177.0 0.3 fusion.24
  177.4 1.1 copy.109
  178.5 1.6 convert_add_fusion
  180.2 1.9 copy.108
  182.0 0.5 select_reduce_fusion
  182.5 10.9 %slice.36 = bf16[3072,2048]{1,0:T(8,128)(2,1)} slice(bf16[3072,2176]{1,0:T(8,128)(2,1)} %all-gather.2.cloned.1.call-done), slice={[0:3072], [0:2048]} | slice | bytes 25165824 | tf_op jit(solution)/shard_map/slice | solution.py:217
  193.5 12.6 %convolution_convert_fusion = bf16[32,96,2048]{2,1,0:T(8,128)(2,1)} fusion(pred[32,96,96]{1,2,0:T(32,128)(4,1)S(1)} %copy.109, bf16[32,96,2048]{2,1,0:T(8,128)(2,1)} %bitcast.92), kind=kOutput, calls=%fused_computation.10 | convolution fusion | flops 1214251008 | bytes 25460736 | tf_op jit(solution)/shard_map/bsr,brd->bsd/dot_general | solution.py:232
  206.1 14.5 %copy.106 = bf16[32,96,2048]{2,0,1:T(8,128)(2,1)} copy(bf16[32,96,2048]{2,1,0:T(8,128)(2,1)} %convolution_convert_fusion) | data formatting | bytes 25165824 | tf_op jit(solution)/shard_map/convert_element_type | solution.py:233
  220.6 22.3 %fusion.15 = f32[32,8,12,2,352]{4,0,3,2,1:T(8,128)} fusion(bf16[32,8,12,2048,1]{3,0,4,2,1:T(8,128)(2,1)} %bitcast.95, bf16[8,2048,2,352]{1,3,2,0:T(8,128)(2,1)} %param.14), kind=kOutput, calls=%fused_computation.15 | convolution fusion | flops 8858370048 | bytes 44302336 | tf_op jit(solution)/shard_map/bend,edgf->bengf/dot_general | solution.py:234
  242.9 15.4 %fusion.1 = bf16[32,8,12,2048]{3,0,2,1:T(8,128)(2,1)} fusion(f32[32,8,12]{0,2,1:T(8,128)S(1)} %select_reduce_fusion, bf16[8,352,2048]{2,1,0:T(8,128)(2,1)} %param.15, f32[32,8,12,2,352]{4,0,3,2,1:T(8,128)} %fusion.15), kind=kOutput, calls=%fused_computation.2 | convolution fusion | flops 4448256000 | bytes 32780288 | tf_op jit(solution)/shard_map/benf,efd->bend/dot_general | solution.py:236
  258.3 25.2 %fusion.10 = bf16[32,96,2048]{2,1,0:T(8,128)(2,1)} fusion(pred[32,96,96]{1,2,0:T(32,128)(4,1)S(1)} %copy.109, bf16[32,96,2048]{2,0,1:T(8,128)(2,1)} %bitcast.94), kind=kOutput, calls=%fused_computation.9 | convolution fusion | flops 1214251008 | bytes 25460736 | tf_op jit(solution)/shard_map/bsr,bsd->brd/dot_general | solution.py:238
  283.5 81.0 %shard_map.82 = f32[96,2048]{1,0:T(8,128)S(1)} custom-call(bf16[8,4,96,2048]{3,2,1,0:T(8,128)(2,1)} %bitcast.93), custom_call_target="tpu_custom_call" | custom-call | tf_op jit(solution)/shard_map/pallas_call | solution.py:160
  364.5 0.9 fusion.30
  365.4 0.0 copy-done.1
  (14 shorter events, 0.1 us)
Async XLA Ops:
  6.5 30.5 %copy-start = (bf16[512,2048]{1,0:T(8,128)(2,1)S(1)}, bf16[512,2048]{1,0:T(8,128)(2,1)}, u32[]{:S(2)}) copy-start(bf16[512,2048]{1,0:T(8,128)(2,1)} %param.10) | copy-start | bytes 6291460
  6.5 63.5 %reduce-scatter.2.cloned.1.call-start = ((), (), s32[]{:S(2)}) async-start(), calls=%async_computation.2 | async-start | bytes 1966080 | tf_op jit(solution)/shard_map/reduce_scatter | solution.py:206
  30.5 4.4 %copy-start.4 = (bf16[384,1,1,512]{0,3,2,1:T(8,128)(2,1)S(1)}, bf16[384,1,1,512]{0,3,2,1:T(8,128)(2,1)}, u32[]{:S(2)}) copy-start(bf16[384,1,1,512]{0,3,2,1:T(8,128)(2,1)} %copy.97) | copy-start | bytes 1179652
  37.0 33.1 %copy-start.2 = (bf16[1,96,2048]{2,1,0:T(8,128)(2,1)S(1)}, bf16[1,96,2048]{2,1,0:T(8,128)(2,1)}, u32[]{:S(2)}) copy-start(bf16[1,96,2048]{2,1,0:T(8,128)(2,1)} %param.8) | copy-start | bytes 1179652
  37.0 34.3 %copy-start.5 = (f32[2048]{0:T(1024)S(1)}, f32[2048]{0:T(1024)}, u32[]{:S(2)}) copy-start(f32[2048]{0:T(1024)} %param.11) | copy-start | bytes 24580
  37.0 35.4 %copy-start.6 = (bf16[2048,64]{0,1:T(8,128)(2,1)S(1)}, bf16[2048,64]{0,1:T(8,128)(2,1)}, u32[]{:S(2)}) copy-start(bf16[2048,64]{0,1:T(8,128)(2,1)} %param.12) | copy-start | bytes 786436
  39.2 134.3 %all-gather.2.cloned.1.call-start = ((), (), s32[]{:S(2)}) async-start(), calls=%async_computation.3 | async-start | bytes 13787136 | tf_op jit(solution)/shard_map/all_gather | solution.py:216
  283.5 81.9 %copy-start.1 = (bf16[512,2048]{1,0:T(8,128)(2,1)S(1)}, bf16[512,2048]{1,0:T(8,128)(2,1)}, u32[]{:S(2)}) copy-start(bf16[512,2048]{1,0:T(8,128)(2,1)} %param.10) | copy-start | bytes 6291460
  283.5 81.0 %copy-start.3 = (bf16[96,2048]{1,0:T(8,128)(2,1)S(1)}, bf16[96,2048]{1,0:T(8,128)(2,1)}, u32[]{:S(2)}) copy-start(bf16[96,2048]{1,0:T(8,128)(2,1)} %reduce-scatter.2.cloned.1.call-done) | copy-start | bytes 1179652
Sparse Core Ops, SparseCore 0:
  39.4 30.6 reduce-scatter.1
  73.9 99.5 all-gather.1
